TPU v7x, 256 devices: a whole 4x4x8 slice. The times are simulated.
256 devices in a mesh: sub: 32 (over x, y, core), grp: 8 (over z).
Axes of the slice: x: 4, y: 4, z: 8, core: 2. Of those that a mesh axis runs over, the one named last changes fastest.
Arguments:
- residual: float32 [256, 1024, 256], P(('sub', 'grp')), may hold values from -6 to 6
- dscale: float32 [256, 1024], P(('sub', 'grp')), may hold values from 0.3 to 1
- local_inverse: bfloat16 [256, 1024, 1024], P(('sub', 'grp')), may hold values from -4 to 4
- coarse_basis: bfloat16 [256, 1024, 384], P(('sub', 'grp')), may hold values from -0.1875 to 0.1875
- block_counts: int32 [256], P(('sub', 'grp')), may hold values from 1 to 3, as said below
- block_index: int32 [256, 3], P(('sub', 'grp')), may hold values from 0 to 11, as said below
- level2_inverse: bfloat16 [32, 1536, 1536], P('sub', 'grp'), may hold values from -4 to 4
- level2_basis: bfloat16 [32, 1536, 1024], P('sub', 'grp'), may hold values from -0.15625 to 0.15625
- group_index: int32 [32, 8], P('sub'), may hold values from 0 to 31, as said below
- level3_inverse: bfloat16 [4096, 4096], P(('sub', 'grp')), may hold values from -4 to 4
Outputs:
- result: float32 [256, 1024, 256], P(('sub', 'grp'))
Inputs may be any that keep to these rules, and one draw needn't show every extreme that they name: `block_counts`: each level-2 subdomain has at least one member with all 3 blocks live. `block_index`: the blocks of one subdomain name different level-2 blocks; before block_counts are applied, the subdomains of one level-2 subdomain name each of its blocks exactly 8 * 3 / 12 times. `group_index`: the blocks of one level-2 subdomain name different level-3 blocks; all level-2 subdomains together name each level-3 block exactly 32 * 8 / 32 times.
All inputs are finite; a program needn't handle non-finite values.
Results may differ from a plain program's by a relative error of at most 0.0035.
Values may be sent and summed in bfloat16 or wider, within the bound.
A program may use at most 64 MiB of HBM per device.

v0:
```python
import jax
import jax.numpy as jnp
from jax import lax
from jax.sharding import PartitionSpec as P

CB = 128
NCB = 3
NB2 = 12
MB2 = 8
NB3 = 32


HIGHEST_PRECISION = lax.Precision.HIGHEST


def padded(value, sides, width):
    for axis, dim in sides:
        size, length = (lax.axis_size(axis), value.shape[dim])
        up = [(i, (i + 1) % size) for i in range(size - 1)]
        down = [(j, i) for i, j in up]
        last = lax.slice_in_dim(value, length - width, length, axis=dim)
        first = lax.slice_in_dim(value, 0, width, axis=dim)
        before = lax.ppermute(last, axis, up)
        after = lax.ppermute(first, axis, down)
        value = jnp.concatenate([before, value, after], axis=dim)
    return value


def local(
    residual,
    dscale,
    local_inverse,
    coarse_basis,
    block_counts,
    block_index,
    level2_inverse,
    level2_basis,
    group_index,
    level3_inverse,
):
    local_rows = residual.shape[1]
    columns = residual.shape[2]
    member = lax.axis_index("grp")
    weighted = (dscale[0][:, None] * residual[0]).astype(jnp.bfloat16)
    local_part = jnp.dot(local_inverse[0], weighted, preferred_element_type=jnp.float32)
    coarse = lax.dot_general(
        coarse_basis[0], weighted, (((0,), (0,)), ((), ())), preferred_element_type=jnp.float32
    )
    active = jnp.arange(NCB, dtype=jnp.int32) < block_counts[0]
    blocks = coarse.reshape(NCB, CB, columns) * active[:, None, None].astype(jnp.float32)
    slot_ids = jnp.arange(NB2, dtype=jnp.int32)
    all_blocks, all_index, all_counts = (
        lax.all_gather(blocks[None], "grp", axis=0, tiled=True),
        lax.all_gather(block_index, "grp", axis=0, tiled=True),
        lax.all_gather(block_counts, "grp", axis=0, tiled=True),
    )
    member_active = jnp.arange(NCB, dtype=jnp.int32)[None, :] < all_counts[:, None]
    slot_table = (
        (all_index[:, :, None] == slot_ids[None, None, :]) & member_active[:, :, None]
    ).astype(jnp.float32)
    level2_rhs = jnp.einsum("mkj,mkcr->jcr", slot_table, all_blocks, precision=HIGHEST_PRECISION)
    level2_b = level2_rhs.reshape(NB2 * CB, columns).astype(jnp.bfloat16)
    own_rows = level2_inverse.shape[1]
    level2_local = jnp.dot(level2_inverse[0], level2_b, preferred_element_type=jnp.float32)
    mine_rhs = lax.dynamic_slice_in_dim(level2_b, member * own_rows, own_rows, 0)
    basis_rows = level2_basis[0]
    level2_coarse = lax.psum_scatter(
        lax.dot_general(
            basis_rows, mine_rhs, (((0,), (0,)), ((), ())), preferred_element_type=jnp.float32
        ),
        "grp",
        scatter_dimension=0,
        tiled=True,
    )
    own_blocks = level2_coarse.shape[0] // CB
    own_groups = lax.dynamic_slice_in_dim(group_index[0], member * own_blocks, own_blocks, 0)
    group_table = (own_groups[:, None] == jnp.arange(NB3, dtype=jnp.int32)[None, :]).astype(
        jnp.float32
    )
    level3_part = jnp.einsum(
        "tb,tcr->bcr",
        group_table,
        level2_coarse.reshape(own_blocks, CB, columns),
        precision=HIGHEST_PRECISION,
    )
    level3_rhs = lax.psum(level3_part, ("sub", "grp"))
    level3_b = level3_rhs.reshape(NB3 * CB, columns).astype(jnp.bfloat16)
    level3_rows = jnp.dot(level3_inverse, level3_b, preferred_element_type=jnp.float32).astype(
        jnp.bfloat16
    )
    level3_solution = lax.all_gather(level3_rows, ("sub", "grp"), axis=0, tiled=True)
    level3_taken = level3_solution.reshape(NB3, CB, columns)[group_index[0]].reshape(
        MB2 * CB, columns
    )
    level2_rows = (
        level2_local + jnp.dot(basis_rows, level3_taken, preferred_element_type=jnp.float32)
    ).astype(jnp.bfloat16)
    level2_solution = lax.all_gather(level2_rows, "grp", axis=0, tiled=True)
    chosen = level2_solution.reshape(NB2, CB, columns)[block_index[0]]
    chosen = jnp.where(active[:, None, None], chosen, jnp.zeros_like(chosen))
    coarse_part = jnp.dot(
        coarse_basis[0], chosen.reshape(NCB * CB, columns), preferred_element_type=jnp.float32
    )
    total = dscale[0][:, None] * (local_part + coarse_part)
    face_width = local_rows // 8
    lower_grp = total[0:face_width]
    upper_grp = total[face_width : 2 * face_width]
    lower_sub = total[2 * face_width : 3 * face_width]
    upper_sub = total[3 * face_width : 4 * face_width]
    grp_padded = padded(jnp.stack([lower_grp, upper_grp]), (("grp", 0),), 1)
    sub_padded = padded(jnp.stack([lower_sub, upper_sub]), (("sub", 0),), 1)
    result = jnp.concatenate(
        [
            lower_grp + grp_padded[0],
            upper_grp + grp_padded[3],
            lower_sub + sub_padded[0],
            upper_sub + sub_padded[3],
            total[4 * face_width :],
        ],
        axis=0,
    )
    return result[None]


def solution(mesh):
    return jax.shard_map(
        local,
        mesh=mesh,
        in_specs=(
            P(("sub", "grp"), None, None),
            P(("sub", "grp"), None),
            P(("sub", "grp"), None, None),
            P(("sub", "grp"), None, None),
            P(("sub", "grp")),
            P(("sub", "grp"), None),
            P("sub", "grp", None),
            P("sub", "grp", None),
            P("sub", None),
            P(("sub", "grp"), None),
        ),
        out_specs=P(("sub", "grp"), None, None),
        check_vma=False,
    )
```

profile of v0, /device:TPU:1, one launch (start us, length us, event | category | flops | bytes accessed | tf_op | source)
XLA Modules:
  0.0 400.5 jit_solution(16217870453562896547)
XLA Ops:
  6.5 2.4 convolution_bitcast_fusion.1
  12.2 14.0 %all-reduce = s32[8]{0:T(128)S(1)} all-reduce(s32[8]{0:T(128)S(1)} %dynamic-update-slice), channel_id=1, replica_groups=mesh['sub'=32,'grp'=8] {'grp'}, use_global_device_ids=true, to_apply=%add | all-reduce | flops 8 | bytes 64
  26.2 12.0 %all-gather = s32[8,1,3]{2,1,0:T(1,128)S(1)} all-gather(s32[1,1,3]{2,1,0:T(1,128)S(1)} %bitcast.102), channel_id=1, replica_groups=mesh['sub'=32,'grp'=8] {'grp'}, dimensions={0}, use_global_device_ids=true | all-gather | bytes 108 | tf_op jit(solution)/shard_map/all_gather | solution.py:54
  38.4 21.0 %all-gather.4.cloned.1.call-done = f32[8,3,128,256]{3,2,1,0:T(8,128)} async-done(((f32[1,3,128,256]{3,2,1,0:T(8,128)}), f32[8,3,128,256]{3,2,1,0:T(8,128)}) %all-gather.4.cloned.1.call-update) | async-done | bytes 3145744 | tf_op jit(solution)/shard_map/all_gather | solution.py:53
  59.4 4.9 %bitcast_convert_fusion = bf16[12,128,256]{2,0,1:T(8,128)(2,1)S(1)} fusion(f32[8,3,128,256]{3,2,1,0:T(8,128)} %all-gather.4.cloned.1.call-done, s32[8,3]{0,1:T(4,128)S(1)} %bitcast.101, pred[8,3]{0,1:T(4,128)(4,1)S(1)} %iota_compare_fusion.1), kind=kOutput, calls=%fused_computation.4 | convolution fusion | flops 113640000 | bytes 3932280 | tf_op jit(solution)/shard_map/mkj,mkcr->jcr/dot_general | solution.py:61
  65.5 1.3 convolution_bitcast_fusion
  68.1 31.9 %reduce-scatter.2.cloned.1.call-done = f32[128,256]{0,1:T(8,128)} async-done(((f32[1024,256]{0,1:T(8,128)}), f32[128,256]{0,1:T(8,128)}) %reduce-scatter.2.cloned.1.call-update) | async-done | bytes 131088 | tf_op jit(solution)/shard_map/reduce_scatter | solution.py:67
  101.0 2.5 broadcast_multiply_fusion
  103.5 133.1 %all-reduce.2 = bf16[32,128,256]{2,1,0:T(8,128)(2,1)} all-reduce(f32[32,128,256]{2,1,0:T(8,128)} %broadcast_multiply_fusion), channel_id=1, replica_groups=mesh['sub'=32,'grp'=8] {'sub','grp'}, use_global_device_ids=true, to_apply=%region_1.0 | all-reduce | flops 1048576 | bytes 6291456 | tf_op jit(solution)/shard_map/psum | solution.py:86
  236.6 2.7 fusion.10
  239.5 2.0 fusion.2
  241.4 1.0 fusion.13
  242.4 100.3 %all-gather.6.cloned.1.call-done = bf16[4096,256]{1,0:T(8,128)(2,1)} async-done(((bf16[16,256]{1,0:T(8,128)(2,1)}), bf16[4096,256]{1,0:T(8,128)(2,1)}) %all-gather.6.cloned.1.call-update) | async-done | bytes 2097168 | tf_op jit(solution)/shard_map/all_gather | solution.py:91
  342.7 3.0 gather_fusion
  345.7 1.4 fusion.9
  347.1 22.9 %all_gather.19 = bf16[1536,256]{1,0:T(8,128)(2,1)} all-gather(bf16[192,256]{1,0:T(8,128)(2,1)S(1)} %fusion.9), channel_id=1, replica_groups=mesh['sub'=32,'grp'=8] {'grp'}, dimensions={0}, use_global_device_ids=true | all-gather | bytes 884736 | tf_op jit(solution)/shard_map/all_gather | solution.py:98
  369.9 1.7 gather_fusion.1
  371.7 1.6 fusion.7
  373.4 2.9 collective-permute-start
  376.3 1.3 collective-permute-start.1
  377.6 8.7 %collective-permute-start.2 = (f32[1,128,256]{1,2,0:T(8,128)S(1)}, f32[1,128,256]{1,2,0:T(8,128)S(1)}, u32[]{:S(2)}, u32[]{:S(2)}) collective-permute-start(f32[1,128,256]{1,2,0:T(8,128)S(1)} %get-tuple-element.7), channel_id=1, source_target_pairs={{0,8},{8,16},{16,24},{24,32},{32,40},{40,48},{48,56},{56,64},{64,7... | collective-permute-start | bytes 393224 | tf_op jit(solution)/shard_map/ppermute | solution.py:23
  386.3 1.9 collective-permute-start.3
  388.4 4.2 %collective-permute-done.3 = f32[1,128,256]{1,2,0:T(8,128)S(1)} collective-permute-done((f32[1,128,256]{1,2,0:T(8,128)S(1)}, f32[1,128,256]{1,2,0:T(8,128)S(1)}, u32[]{:S(2)}, u32[]{:S(2)}) %collective-permute-start.3) | collective-permute-done | bytes 131104 | tf_op jit(solution)/shard_map/ppermute | solution.py:24
  392.7 1.3 copy.26
  (55 shorter events, 6.4 us)
Async XLA Ops:
  6.5 232.9 %copy-start = (bf16[1,1024,1024]{2,1,0:T(8,128)(2,1)S(1)}, bf16[1,1024,1024]{2,1,0:T(8,128)(2,1)}, u32[]{:S(2)}) copy-start(bf16[1,1024,1024]{2,1,0:T(8,128)(2,1)} %param.12) | copy-start | bytes 6291460
  6.5 52.9 %all-gather.4.cloned.1.call-start = ((), (), s32[]{:S(2)}) async-start(), calls=%async_computation.1 | async-start | bytes 3538944 | tf_op jit(solution)/shard_map/all_gather | solution.py:53
  6.5 4.2 %copy-start.10 = (u32[256]{0:T(256)S(1)}, u32[256]{0:T(256)}, u32[]{:S(2)}) copy-start(u32[256]{0:T(256)} %constant.33) | copy-start | bytes 3076
  6.5 19.7 %copy-start.8 = (s32[1,3]{1,0:T(1,128)S(1)}, s32[1,3]{1,0:T(1,128)}, u32[]{:S(2)}) copy-start(s32[1,3]{1,0:T(1,128)} %param.15) | copy-start | bytes 40
  10.6 89.4 %reduce-scatter.2.cloned.1.call-start = ((), (), s32[]{:S(2)}) async-start(), calls=%async_computation.2 | async-start | bytes 1179648 | tf_op jit(solution)/shard_map/reduce_scatter | solution.py:67
  59.4 6.1 %copy-start.5 = (bf16[1,192,1024]{2,1,0:T(8,128)(2,1)S(1)}, bf16[1,192,1024]{2,1,0:T(8,128)(2,1)}, u32[]{:S(2)}) copy-start(bf16[1,192,1024]{2,1,0:T(8,128)(2,1)} %param.17) | copy-start | bytes 1179652
  64.3 2.5 copy-start.9
  64.6 0.9 copy-start.3
  66.8 275.9 %all-gather.6.cloned.1.call-start = ((), (), s32[]{:S(2)}) async-start(), calls=%async_computation.3 | async-start | bytes 2105344 | tf_op jit(solution)/shard_map/all_gather | solution.py:91
  236.6 2.8 copy-start.1
  236.6 2.8 copy-start.7
  239.4 2.0 copy-start.4
  239.5 2.0 copy-start.6
  242.4 129.3 %copy-start.2 = (f32[256,1024]{1,0:T(8,128)S(1)}, f32[256,1024]{1,0:T(8,128)}, u32[]{:S(2)}) copy-start(f32[256,1024]{1,0:T(8,128)} %fusion.2) | copy-start | bytes 3145732
  373.4 14.9 %collective-permute-start = (f32[1,128,256]{1,2,0:T(8,128)S(1)}, f32[1,128,256]{1,2,0:T(8,128)S(1)}, u32[]{:S(2)}, u32[]{:S(2)}) collective-permute-start(f32[1,128,256]{1,2,0:T(8,128)S(1)} %get-tuple-element.8), channel_id=1, source_target_pairs={{0,1},{1,2},{2,3},{3,4},{4,5},{5,6},{6,7},{8,9},{9,10},{10,11},{11... | collective-permute-start | bytes 393224 | tf_op jit(solution)/shard_map/ppermute | solution.py:23
  376.3 12.0 %collective-permute-start.1 = (f32[1,128,256]{1,2,0:T(8,128)S(1)}, f32[1,128,256]{1,2,0:T(8,128)S(1)}, u32[]{:S(2)}, u32[]{:S(2)}) collective-permute-start(f32[1,128,256]{1,2,0:T(8,128)S(1)} %get-tuple-element.6), channel_id=1, source_target_pairs={{1,0},{2,1},{3,2},{4,3},{5,4},{6,5},{7,6},{9,8},{10,9},{11,10},{12... | collective-permute-start | bytes 393224 | tf_op jit(solution)/shard_map/ppermute | solution.py:24
  377.6 10.8 %collective-permute-start.2 = (f32[1,128,256]{1,2,0:T(8,128)S(1)}, f32[1,128,256]{1,2,0:T(8,128)S(1)}, u32[]{:S(2)}, u32[]{:S(2)}) collective-permute-start(f32[1,128,256]{1,2,0:T(8,128)S(1)} %get-tuple-element.7), channel_id=1, source_target_pairs={{0,8},{8,16},{16,24},{24,32},{32,40},{40,48},{48,56},{56,64},{64,7... | collective-permute-start | bytes 393224 | tf_op jit(solution)/shard_map/ppermute | solution.py:23
  386.3 6.3 %collective-permute-start.3 = (f32[1,128,256]{1,2,0:T(8,128)S(1)}, f32[1,128,256]{1,2,0:T(8,128)S(1)}, u32[]{:S(2)}, u32[]{:S(2)}) collective-permute-start(f32[1,128,256]{1,2,0:T(8,128)S(1)} %get-tuple-element.5), channel_id=1, source_target_pairs={{8,0},{16,8},{24,16},{32,24},{40,32},{48,40},{56,48},{64,56},{72,6... | collective-permute-start | bytes 393224 | tf_op jit(solution)/shard_map/ppermute | solution.py:24
Sparse Core Ops, SparseCore 0:
  10.8 48.5 all-gather.3
  67.0 33.0 reduce-scatter.1
  239.5 103.1 all-gather.5
where the time goes:
time: 403 us; the launch traced here: 401 us
  blocking collectives  182 us (45%)
  waiting for transfers between devices  158 us (39%)
  matrix products  17.3 us (4%)
  starting transfers between devices  14.9 us (4%)
  between operations  14.1 us (3%)
  local copies, waits for them, and re-layouts  10.6 us (3%)
  other arithmetic  4.18 us (1%)
    psum x1, blocking collectives, local(): level3_rhs = lax.psum(level3_part, ('sub', 'grp'))  133 us
    all_gather x1, waiting for transfers between devices, local(): lax.all_gather(level3_rows, ('sub', 'grp'), axis=0, tiled=True)  100 us
    reduce_scatter x1, waiting for transfers between devices, local(): lax.psum_scatter(lax.dot_general(basis_rows, mine_rhs, (((0,), (0,)), (()...  31.9 us
    all_gather x1, blocking collectives, local(): level2_solution = lax.all_gather(level2_rows, 'grp', axis=0, tiled=True)  22.9 us
    all_gather x1, waiting for transfers between devices, local(): lax.all_gather(blocks[None], 'grp', axis=0, tiled=True)  21 us
    unnamed x1, blocking collectives  14 us
    all_gather x1, blocking collectives, local(): lax.all_gather(block_index, 'grp', axis=0, tiled=True)  12 us
    ppermute x2, starting transfers between devices, padded(): before = lax.ppermute(last, axis, up)  11.6 us
  transfers between devices with their start and end apart: 7, of which 4 were waited for; matrix products, arithmetic and copies ran while one was open for 1% of the time, Pallas kernels for 0%

commit v1 on v0

v1 whole, which is shorter than its diff:
```python
import functools

import jax
import jax.numpy as jnp
from jax import lax
from jax.experimental import pallas as pl
from jax.experimental.pallas import tpu as pltpu
from jax.sharding import PartitionSpec as P

NS = 32
NG = 8
NL = 1024
NR = 256
CB = 128
NCB = 3
NB2 = 12
MB2 = 8
NB3 = 32
SL = CB // NG
OWN2 = NB2 * CB // NG
HB = CB // 2
NH = OWN2 // HB
NCH = 1
W = NR // NCH
NSUB = 3

MESH = pl.DeviceIdType.MESH
BF = jnp.bfloat16
F32 = jnp.float32


def dot(a, b):
    return jnp.dot(a, b, preferred_element_type=F32)


def dot_t(a, b):
    return lax.dot_general(a, b, (((0,), (0,)), ((), ())), preferred_element_type=F32)


def kernel(
    cnt_s, bidx_s, gidx_s, dsc_v, res_h, linv_h, cbas_h, l2inv_h, l2bas_h, l3inv_h,
    out_ref,
    res, linv, cbas, l2inv, l2bas, l3inv, load_sem,
    dcol, wgt, local, perm, tstage, tsend, tile, t_ss, t_rs,
    meta_v, meta_s, m_ss, m_rs, ms_sem, tab, gtab,
    blocks, b_ss, b_rs,
    rhs2, l2loc, part, d_recv, d_ss, d_rs,
    ssum, dense, e_recv, e_ss, e_rs,
    xall, f_ss, f_rs,
    hsend, h_recv, h_ss, h_rs,
    yall, i_ss, i_rs,
    picked, lifted, j_ss, j_rs,
    sol2, l_ss, l_rs,
    chosen, fsend, f_recv, n_ss, n_rs,
):
    s, g = lax.axis_index("sub"), lax.axis_index("grp")

    loads = [
        pltpu.make_async_copy(src, dst, load_sem.at[n])
        for n, (src, dst) in enumerate(
            [(res_h, res), (cbas_h, cbas), (linv_h, linv), (l2bas_h, l2bas), (l2inv_h, l2inv),
             (l3inv_h, l3inv)]
        )
    ]
    for load in loads:
        load.start()

    bar = pltpu.get_barrier_semaphore()

    def hail_z(i, c):
        pl.semaphore_signal(bar, inc=1, device_id=(s, lax.rem(g + i, NG)), device_id_type=MESH)
        return c

    def hail_p(i, c):
        pl.semaphore_signal(bar, inc=1, device_id=(lax.rem(s + i, NS), g), device_id_type=MESH)
        return c

    lax.fori_loop(1, NG, hail_z, 0)
    lax.fori_loop(1, NS, hail_p, 0)

    def remote(src, dst, ss, rs, dev):
        return pltpu.make_async_remote_copy(
            src_ref=src, dst_ref=dst, send_sem=ss, recv_sem=rs, device_id=dev, device_id_type=MESH
        )

    def z_copy(i, make, ss, rs):
        t = lax.rem(g + i, NG)
        src, dst = make(t)
        return remote(src, dst, ss.at[i], rs.at[i], (s, t))

    def p_copy(i, make, ss, rs):
        t = lax.rem(s + i, NS)
        src, dst = make(t)
        return remote(src, dst, ss.at[i], rs.at[i], (t, g))

    def start_all(copy, n, make, ss, rs):
        def f(i, c):
            copy(i, make, ss, rs).start()
            return c

        lax.fori_loop(1, n, f, 0)

    def recv_all(copy, n, make, ss, rs):
        def f(i, c):
            copy(i, make, ss, rs).wait_recv()
            return c

        lax.fori_loop(1, n, f, 0)

    def sent_all(copy, n, make, ss, rs):
        def f(i, c):
            copy(i, make, ss, rs).wait_send()
            return c

        lax.fori_loop(1, n, f, 0)

    def ring_copy(way, step, q, slot, ss, rs):
        if way == 0:
            o, t = lax.rem(g - step + NG, NG), lax.rem(g + 1, NG)
        else:
            o, t = lax.rem(g + step, NG), lax.rem(g + NG - 1, NG)
        ref = slot(o, q)
        return remote(ref, ref, ss.at[way, step, q], rs.at[way, step, q], (s, t))

    half = NG // 2

    def ring_steps():
        for step in range(half):
            for q in range(NSUB):
                for way in range(2):
                    if step == half - 1 and (q % 2 != way):
                        continue
                    yield step, q, way

    def ring(slot, ss, rs):
        for step, q, way in ring_steps():
            if step > 0:
                ring_copy(way, step - 1, q, slot, ss, rs).wait_recv()
            ring_copy(way, step, q, slot, ss, rs).start()

    def ring_end(slot, ss, rs):
        for q in range(NSUB):
            for way in range(2):
                last = half - 1 if q % 2 == way else half - 2
                ring_copy(way, last, q, slot, ss, rs).wait_recv()

    def ring_sent(slot, ss, rs):
        for step, q, way in ring_steps():
            ring_copy(way, step, q, slot, ss, rs).wait_send()

    def spread(i, c):
        at = pl.ds(pl.multiple_of(i * 128, 128), 128)
        row = jnp.broadcast_to(dsc_v[0:1, at], (128, 128))
        dcol[at, :] = row.T
        return c

    lax.fori_loop(0, NL // 128, spread, 0)
    loads[0].wait()

    def weigh(i, c):
        at = pl.ds(pl.multiple_of(i * 128, 128), 128)
        d = dcol[at, :]
        for n in range(NR // 128):
            cols = slice(n * 128, n * 128 + 128)
            wgt[at, cols] = (res[at, cols] * d).astype(BF)
        return c

    lax.fori_loop(0, NL // 128, weigh, 0)

    lane = lax.broadcasted_iota(jnp.int32, (1, 128), 1)
    meta_v[pl.ds(g, 1), :] = jnp.where(
        lane == 0, bidx_s[0, 0], jnp.where(lane == 1, bidx_s[0, 1], bidx_s[0, 2])
    )
    pl.semaphore_wait(bar, NG - 1 + NS - 1)

    def m_make(t):
        return meta_v.at[pl.ds(g, 1)], meta_v.at[pl.ds(g, 1)]

    start_all(z_copy, NG, m_make, m_ss, m_rs)

    loads[1].wait()
    for c in range(NCH):
        for k in range(NCB):
            v = dot_t(cbas[:, k * CB : (k + 1) * CB], wgt[:, c * W : (c + 1) * W])
            live = (cnt_s[0] > k).astype(F32)
            blocks[c, pl.ds((g * NCB + k) * 2, 2)] = (v * live).astype(BF).reshape(2, HB, W)

    def b_slot(c):
        return lambda o, q: blocks.at[c, pl.ds((o * NCB + q) * 2, 2)]

    for c in range(NCH):
        ring(b_slot(c), b_ss.at[c], b_rs.at[c])

    loads[2].wait()

    def local_tile(i, c):
        at = pl.ds(pl.multiple_of(i * 256, 256), 256)
        local[at, :] = dot(linv[at, :], wgt[...])
        return c

    lax.fori_loop(0, NL // 256, local_tile, 0)

    recv_all(z_copy, NG, m_make, m_ss, m_rs)
    to_s = pltpu.make_async_copy(meta_v, meta_s, ms_sem)
    to_s.start()
    to_s.wait()

    def name_pairs(j, c):
        lo = jnp.int32(NG * NCB - 1)
        hi = jnp.int32(0)
        for p in range(NG * NCB - 1, -1, -1):
            lo = jnp.where(meta_s[p // NCB, p % NCB] == j, p, lo)
        for p in range(NG * NCB):
            hi = jnp.where(meta_s[p // NCB, p % NCB] == j, p, hi)
        tab[0, j] = lo
        tab[1, j] = hi
        return c

    lax.fori_loop(0, NB2, name_pairs, 0)

    def name_slots(b, c):
        at = jnp.int32(0)
        has = jnp.int32(0)
        for j in range(MB2):
            hit = gidx_s[0, j] == b
            at = jnp.where(hit, j, at)
            has = jnp.where(hit, 1, has)
        gtab[0, b] = at
        gtab[1, b] = has
        return c

    lax.fori_loop(0, NB3, name_slots, 0)

    loads[5].wait()
    for q in range(4):
        tstage[q * SL : (q + 1) * SL, :] = l3inv[:, q * 1024 : (q + 1) * 1024]

    def fill_perm(b, c):
        k = lax.broadcasted_iota(jnp.int32, (128, 1024), 0)
        n = lax.broadcasted_iota(jnp.int32, (128, 1024), 1)
        want = (k // SL) * 128 + b * SL + k % SL
        perm[pl.ds(pl.multiple_of(b * 128, 128), 128), :] = jnp.where(n == want, 1.0, 0.0).astype(BF)
        return c

    lax.fori_loop(0, 8, fill_perm, 0)
    moved = dot(tstage[...], perm[...]).astype(BF)
    for m in range(NG):
        for q in range(4):
            tsend[m, :, q * 128 : (q + 1) * 128] = moved[q * SL : (q + 1) * SL, m * 128 : (m + 1) * 128]

    def t_make(t):
        return tsend.at[t], tile.at[g]

    tile[g] = tsend[g]
    start_all(z_copy, NG, t_make, t_ss, t_rs)

    loads[3].wait()
    loads[4].wait()

    def own_rhs(c):
        ring_end(b_slot(c), b_ss.at[c], b_rs.at[c])
        pieces = []
        for i in range(3):
            h = g * 3 + i
            j, low = h // 2, lax.rem(h, 2)
            v = blocks[c, tab[0, j] * 2 + low].astype(F32) + blocks[c, tab[1, j] * 2 + low].astype(F32)
            pieces.append(v.astype(BF))
        return jnp.concatenate(pieces, axis=0)

    def d_make(c):
        return lambda t: (part.at[c, :, t], d_recv.at[c, g])

    for c in range(NCH):
        mine = own_rhs(c)
        for n in range(MB2 // 2):
            v = dot_t(l2bas[:, n * 256 : (n + 1) * 256], mine).astype(BF)
            part[c, 2 * n : 2 * n + 2] = v.reshape(2, NG, SL, W)
        start_all(z_copy, NG, d_make(c), d_ss.at[c], d_rs.at[c])
        for j in range(MB2):
            d_recv[c, g, j] = part[c, j, g]

    def sum_pairs(c):
        def f(j, x):
            for low in range(2):
                v = blocks[c, tab[0, j] * 2 + low].astype(F32) + blocks[c, tab[1, j] * 2 + low].astype(F32)
                at = pl.ds(pl.multiple_of(j * CB + low * HB, HB), HB)
                rhs2[at, c * W : (c + 1) * W] = v.astype(BF)
            return x

        lax.fori_loop(0, NB2, f, 0)

    for c in range(NCH):
        sum_pairs(c)
    l2loc[...] = dot(l2inv[...], rhs2[...])

    def e_make(c):
        return lambda t: (dense.at[c, t], e_recv.at[c, s])

    def f_make(c):
        return lambda t: (xall.at[c, s], xall.at[c, s])

    def h_make(c):
        return lambda t: (hsend.at[c, t], h_recv.at[c, g])

    def i_make(c):
        return lambda t: (yall.at[c, s], yall.at[c, s])

    def j_make(c):
        return lambda t: (picked.at[c], lifted.at[c, :, g])

    def l_slot(c):
        return lambda o, q: sol2.at[c, o * NH + q]

    def phase_e(c):
        recv_all(z_copy, NG, d_make(c), d_ss.at[c], d_rs.at[c])
        for j in range(MB2):
            v = d_recv[c, 0, j].astype(F32)
            for m in range(1, NG):
                v = v + d_recv[c, m, j].astype(F32)
            ssum[c, j] = v

        def f(b, x):
            dense[c, b] = (ssum[c, gtab[0, b]] * gtab[1, b].astype(F32)).astype(BF)
            return x

        lax.fori_loop(0, NB3, f, 0)
        start_all(p_copy, NS, e_make(c), e_ss.at[c], e_rs.at[c])
        e_recv[c, s] = dense[c, s]

    def phase_f(c):
        recv_all(p_copy, NS, e_make(c), e_ss.at[c], e_rs.at[c])

        def f(b, v):
            return v + e_recv[c, b].astype(F32)

        xall[c, s] = lax.fori_loop(0, NS, f, jnp.zeros((SL, W), F32)).astype(BF)
        start_all(p_copy, NS, f_make(c), f_ss.at[c], f_rs.at[c])

    def phase_h(c):
        if c == 0:
            recv_all(z_copy, NG, t_make, t_ss, t_rs)
        recv_all(p_copy, NS, f_make(c), f_ss.at[c], f_rs.at[c])
        v = dot(tile[...].reshape(CB, NB3 * SL), xall[c].reshape(NB3 * SL, W))
        hsend[c] = v.astype(BF).reshape(NG, SL, W)
        start_all(z_copy, NG, h_make(c), h_ss.at[c], h_rs.at[c])
        h_recv[c, g] = hsend[c, g]

    def phase_i(c):
        recv_all(z_copy, NG, h_make(c), h_ss.at[c], h_rs.at[c])
        v = h_recv[c, 0].astype(F32)
        for m in range(1, NG):
            v = v + h_recv[c, m].astype(F32)
        yall[c, s] = v.astype(BF)
        start_all(p_copy, NS, i_make(c), i_ss.at[c], i_rs.at[c])

    def phase_j(c):
        recv_all(p_copy, NS, i_make(c), i_ss.at[c], i_rs.at[c])
        for j in range(MB2):
            v = yall[c, gidx_s[0, j]]
            picked[c, j] = v
            lifted[c, j, g] = v
        start_all(z_copy, NG, j_make(c), j_ss.at[c], j_rs.at[c])

    def phase_l(c):
        recv_all(z_copy, NG, j_make(c), j_ss.at[c], j_rs.at[c])
        cols = slice(c * W, (c + 1) * W)
        v = l2loc[:, cols] + dot(l2bas[...], lifted[c].reshape(MB2 * CB, W))
        sol2[c, pl.ds(g * NH, NH)] = v.astype(BF).reshape(NH, HB, W)
        ring(l_slot(c), l_ss.at[c], l_rs.at[c])

    def n_copy(c, f):
        dev = (
            (s, lax.rem(g + NG - 1, NG)),
            (s, lax.rem(g + 1, NG)),
            (lax.rem(s + NS - 1, NS), g),
            (lax.rem(s + 1, NS), g),
        )[f]
        return remote(fsend.at[c, f], f_recv.at[c, f ^ 1], n_ss.at[c, f], n_rs.at[c, f ^ 1], dev)

    def total_rows(c, lo, n):
        v = dot(cbas[lo : lo + n, :], chosen[c])
        cols = slice(c * W, (c + 1) * W)
        v = v + local[lo : lo + n, cols]
        d = dcol[lo : lo + n, :]
        if W > 128:
            d = jnp.concatenate([d] * (W // 128), axis=1)
        return v * d

    def phase_n(c):
        ring_end(l_slot(c), l_ss.at[c], l_rs.at[c])
        for k in range(NCB):
            for low in range(2):
                v = sol2[c, bidx_s[0, k] * 2 + low].astype(F32) * (cnt_s[0] > k).astype(F32)
                at = k * CB + low * HB
                chosen[c, at : at + HB, :] = v.astype(BF)
        cols = slice(c * W, (c + 1) * W)
        for f in range(4):
            v = total_rows(c, f * CB, CB)
            out_ref[f * CB : (f + 1) * CB, cols] = v
            fsend[c, f] = v.astype(BF)
            n_copy(c, f).start()
        for f in range(2, 4):
            out_ref[f * 256 : (f + 1) * 256, cols] = total_rows(c, f * 256, 256)

    def phase_o(c):
        cols = slice(c * W, (c + 1) * W)
        inside = (g > 0, g < NG - 1, s > 0, s < NS - 1)
        for f in range(4):
            n_copy(c, f ^ 1).wait_recv()
            at = slice(f * CB, (f + 1) * CB)
            v = f_recv[c, f].astype(F32) * inside[f].astype(F32)
            out_ref[at, cols] = out_ref[at, cols] + v

    for phase in (phase_e, phase_f, phase_h, phase_i, phase_j, phase_l, phase_n, phase_o):
        for c in range(NCH):
            phase(c)

    sent_all(z_copy, NG, m_make, m_ss, m_rs)
    sent_all(z_copy, NG, t_make, t_ss, t_rs)
    for c in range(NCH):
        ring_sent(b_slot(c), b_ss.at[c], b_rs.at[c])
        sent_all(z_copy, NG, d_make(c), d_ss.at[c], d_rs.at[c])
        sent_all(p_copy, NS, e_make(c), e_ss.at[c], e_rs.at[c])
        sent_all(p_copy, NS, f_make(c), f_ss.at[c], f_rs.at[c])
        sent_all(z_copy, NG, h_make(c), h_ss.at[c], h_rs.at[c])
        sent_all(p_copy, NS, i_make(c), i_ss.at[c], i_rs.at[c])
        sent_all(z_copy, NG, j_make(c), j_ss.at[c], j_rs.at[c])
        ring_sent(l_slot(c), l_ss.at[c], l_rs.at[c])
        for f in range(4):
            n_copy(c, f).wait_send()


def local(
    residual,
    dscale,
    local_inverse,
    coarse_basis,
    block_counts,
    block_index,
    level2_inverse,
    level2_basis,
    group_index,
    level3_inverse,
):
    vm = pltpu.VMEM
    dma = pltpu.SemaphoreType.DMA
    smem = pl.BlockSpec(memory_space=pltpu.SMEM)
    vmem = pl.BlockSpec(memory_space=pltpu.VMEM)
    hbm = pl.BlockSpec(memory_space=pl.ANY)
    ring_sem = dma((NCH, 2, NG // 2, NSUB))
    z_sem = dma((NCH, NG))
    p_sem = dma((NCH, NS))
    scratch = [
        vm((NL, NR), F32), vm((NL, NL), BF), vm((NL, NCB * CB), BF), vm((OWN2, NB2 * CB), BF),
        vm((OWN2, MB2 * CB), BF), vm((SL, NB3 * CB), BF), dma((6,)),
        vm((NL, 128), F32), vm((NL, NR), BF), vm((NL, NR), F32), vm((1024, 1024), BF),
        vm((4 * SL, 1024), BF), vm((NG, SL, NB3 * SL), BF), vm((NG, SL, NB3 * SL), BF),
        dma((NG,)), dma((NG,)),
        vm((NG, 128), jnp.int32), pltpu.SMEM((NG, 128), jnp.int32), dma((NG,)), dma((NG,)),
        dma(()), pltpu.SMEM((2, NB2), jnp.int32), pltpu.SMEM((2, NB3), jnp.int32),
        vm((NCH, NG * NCB * 2, HB, W), BF), ring_sem, ring_sem,
        vm((NB2 * CB, NR), BF), vm((OWN2, NR), F32), vm((NCH, MB2, NG, SL, W), BF),
        vm((NCH, NG, MB2, SL, W), BF), z_sem, z_sem,
        vm((NCH, MB2, SL, W), F32), vm((NCH, NB3, SL, W), BF), vm((NCH, NS, SL, W), BF), p_sem, p_sem,
        vm((NCH, NB3, SL, W), BF), p_sem, p_sem,
        vm((NCH, NG, SL, W), BF), vm((NCH, NG, SL, W), BF), z_sem, z_sem,
        vm((NCH, NB3, SL, W), BF), p_sem, p_sem,
        vm((NCH, MB2, SL, W), BF), vm((NCH, MB2, NG, SL, W), BF), z_sem, z_sem,
        vm((NCH, NG * NH, HB, W), BF), ring_sem, ring_sem,
        vm((NCH, NCB * CB, W), BF), vm((NCH, 4, CB, W), BF), vm((NCH, 4, CB, W), BF),
        dma((NCH, 4)), dma((NCH, 4)),
    ]
    out = pl.pallas_call(
        kernel,
        out_shape=jax.ShapeDtypeStruct((NL, NR), F32),
        in_specs=[smem, smem, smem, vmem] + [hbm] * 6,
        out_specs=vmem,
        scratch_shapes=scratch,
        name="bddc",
        compiler_params=pltpu.CompilerParams(
            collective_id=0, has_side_effects=True, vmem_limit_bytes=48 << 20
        ),
    )(
        block_counts, block_index, group_index, dscale, residual[0], local_inverse[0],
        coarse_basis[0], level2_inverse[0], level2_basis[0], level3_inverse,
    )
    return out[None]


def solution(mesh):
    return jax.shard_map(
        local,
        mesh=mesh,
        in_specs=(
            P(("sub", "grp"), None, None),
            P(("sub", "grp"), None),
            P(("sub", "grp"), None, None),
            P(("sub", "grp"), None, None),
            P(("sub", "grp")),
            P(("sub", "grp"), None),
            P("sub", "grp", None),
            P("sub", "grp", None),
            P("sub", None),
            P(("sub", "grp"), None),
        ),
        out_specs=P(("sub", "grp"), None, None),
        check_vma=False,
    )
```

time: 403 us -> 120 us (0.30)
  blocking collectives: 182 us -> 0 us
  waiting for transfers between devices: 158 us -> 0 us
  Pallas kernels: 0 us -> 109 us
  matrix products: 17.3 us -> 0 us
  starting transfers between devices: 14.9 us -> 0 us
  between operations: 14.1 us -> 0.68 us
  other arithmetic: 4.18 us -> 0 us
    psum x1 -> x0, blocking collectives: 133 us -> none  [local(): level3_rhs = lax.psum(level3_part, ('sub', 'grp'))]
    all_gather x2 -> x0, waiting for transfers between devices: 121 us -> none  [the longest x1 100 us: local(): lax.all_gather(level3_rows, ('sub', 'grp'), axis=0, tiled=True)]
    pallas_call x0 -> x1, Pallas kernels: none -> 109 us  [local(): pl.pallas_call(kernel, out_shape=jax.ShapeDtypeStruct((NL, NR), F32), in_...]
    all_gather x2 -> x0, blocking collectives: 34.9 us -> none  [the longest x1 22.9 us: local(): level2_solution = lax.all_gather(level2_rows, 'grp', axis=0, tiled=True)]
    reduce_scatter x1 -> x0, waiting for transfers between devices: 31.9 us -> none  [local(): lax.psum_scatter(lax.dot_general(basis_rows, mine_rhs, (((0,), (0,)), (()...]
    dot_general x8 -> x0, matrix products: 17.3 us -> none  [the longest x1 4.93 us: local(): jnp.einsum('mkj,mkcr->jcr', slot_table, all_blocks, precision=HIGHEST_PRE...]
    ppermute x4 -> x0, starting transfers between devices: 14.8 us -> none  [the longest x2 11.6 us: padded(): before = lax.ppermute(last, axis, up)]
    unnamed x1 -> x0, blocking collectives: 14 us -> none
  transfers between devices with their start and end apart: 7 -> 0, of which waited for: 4 -> 0; matrix products, arithmetic and copies ran while one was open for 1% -> 0% of each run, Pallas kernels for 0% -> 0%
where the time goes in v1:
time: 120 us
  Pallas kernels  109 us (91%)
  local copies, waits for them, and re-layouts  9.87 us (8%)
    pallas_call x1, Pallas kernels, local(): pl.pallas_call(kernel, out_shape=jax.ShapeDtypeStruct((NL, NR), F32), in_...  109 us
    unnamed x19, local copies, waits for them, and re-layouts  9.87 us

profile of v1, /device:TPU:1, one launch (start us, length us, event | category | flops | bytes accessed | tf_op | source)
XLA Modules:
  0.0 119.9 jit_solution(5382306229991698244)
XLA Ops:
  0.7 0.0 copy-start
  0.7 1.6 %copy-done = bf16[1,1024,1024]{2,1,0:T(8,128)(2,1)S(1)} copy-done((bf16[1,1024,1024]{2,1,0:T(8,128)(2,1)S(1)}, bf16[1,1024,1024]{2,1,0:T(8,128)(2,1)}, u32[]{:S(2)}) %copy-start) | copy-done | bytes 2097176
  2.2 0.0 copy-start.1
  2.2 1.2 %copy-done.1 = f32[1,1024,256]{2,1,0:T(8,128)S(1)} copy-done((f32[1,1024,256]{2,1,0:T(8,128)S(1)}, f32[1,1024,256]{2,1,0:T(8,128)}, u32[]{:S(2)}) %copy-start.1) | copy-done | bytes 1048600
  3.5 0.0 copy-start.2
  3.5 1.1 copy-done.2
  4.6 0.0 copy-start.3
  4.6 1.1 copy-done.3
  5.7 0.0 copy-start.4
  5.7 1.0 copy-done.4
  6.7 0.0 copy-start.5
  6.7 0.9 copy-done.5
  7.6 0.0 copy-start.6
  7.6 0.7 copy-done.6
  8.3 0.0 copy-start.7
  8.3 0.7 copy-done.7
  8.9 0.0 copy-start.8
  8.9 0.7 copy-done.8
  9.6 109.4 %bddc.1 = f32[1024,256]{1,0:T(8,128)S(1)} custom-call(s32[1]{0:T(128)S(6)} %copy.12.cnt_s, s32[1,3]{1,0:T(1,128)S(1)} %copy-done.7, s32[1,8]{1,0:T(1,128)S(1)} %copy-done.8, f32[1,1024]{1,0:T(1,128)S(1)} %copy-done.6, f32[1024,256]{1,0:T(8,128)S(1)} %bitcast.8, bf16[1024,1024]{1,0:T(8,128)(2,1)S(1)} %bitcast.7, bf16[1024,384]{1,0:T(8,128)(2,1)S(1)} %bitcast.9, ...), custom_call_target="tpu_custom_call" | custom-call | tf_op jit(solution)/shard_map/bddc/pallas_call | solution.py:473
  119.0 1.0 copy.13
Async XLA Ops:
  0.7 1.6 %copy-start = (bf16[1,1024,1024]{2,1,0:T(8,128)(2,1)S(1)}, bf16[1,1024,1024]{2,1,0:T(8,128)(2,1)}, u32[]{:S(2)}) copy-start(bf16[1,1024,1024]{2,1,0:T(8,128)(2,1)} %param.12) | copy-start | bytes 6291460
  2.2 1.2 %copy-start.1 = (f32[1,1024,256]{2,1,0:T(8,128)S(1)}, f32[1,1024,256]{2,1,0:T(8,128)}, u32[]{:S(2)}) copy-start(f32[1,1024,256]{2,1,0:T(8,128)} %param.10) | copy-start | bytes 3145732
  3.5 1.1 copy-start.2
  4.6 1.1 copy-start.3
  5.7 1.0 copy-start.4
  6.7 0.9 copy-start.5
  7.6 0.7 copy-start.6
  8.3 0.7 copy-start.7
  8.9 0.7 copy-start.8

commit v2 on v1

v2 whole, which is shorter than its diff:
```python
import functools

import jax
import jax.numpy as jnp
from jax import lax
from jax.experimental import pallas as pl
from jax.experimental.pallas import tpu as pltpu
from jax.sharding import PartitionSpec as P

NS = 32
NG = 8
NL = 1024
NR = 256
CB = 128
NCB = 3
NB2 = 12
MB2 = 8
NB3 = 32
SL = CB // NG
OWN2 = NB2 * CB // NG
HB = CB // 2
NH = OWN2 // HB
NCH = 1
W = NR // NCH
PJ = 2

ORDER = (
    "b0", "w0", "w0", "w0", "w0", "w0", "b0", "w0", "w0", "w0", "d0", "q0", "e0", "t0", "f0", "a0",
    "h0", "a0", "i0", "j0", "g0", "s0", "k0", "l0", "l0", "n0", "r0", "o0",
)

MESH = pl.DeviceIdType.MESH
BF = jnp.bfloat16
F32 = jnp.float32


def dot(a, b):
    return jnp.dot(a, b, preferred_element_type=F32)


def dot_t(a, b):
    return lax.dot_general(a, b, (((0,), (0,)), ((), ())), preferred_element_type=F32)


def kernel(
    cnt_h, bidx_h, gidx_h, dsc_h, res_h, linv_h, cbas_h, l2inv_h, l2bas_h, l3inv_h,
    out_ref,
    cnt_s, bidx_s, gidx_s, dsc_v, res, linv, cbas, l2inv, l2bas, l3inv, load_sem,
    dcol, wgt, local, perm, tstage, tsend, tile, t_ss, t_rs,
    ctab, gtab,
    crs, own, b_stage, b_recv, b_ss, b_rs,
    rhs2, a_ss, a_rs, l2loc, part, d_stage, d_recv, d_ss, d_rs,
    ssum, dense, e_recv, e_ss, e_rs,
    xall, f_ss, f_rs,
    hsend, h_recv, h_ss, h_rs,
    yall, i_ss, i_rs,
    lifted, j_ss, j_rs,
    sol2, l_ss, l_rs,
    chosen, fsend, f_recv, n_ss, n_rs,
):
    s, g = lax.axis_index("sub"), lax.axis_index("grp")

    loads = [
        pltpu.make_async_copy(src, dst, load_sem.at[n])
        for n, (src, dst) in enumerate(
            [(res_h, res), (cbas_h, cbas), (linv_h, linv), (l2bas_h, l2bas), (l2inv_h, l2inv),
             (l3inv_h, l3inv), (dsc_h, dsc_v), (cnt_h, cnt_s), (bidx_h, bidx_s), (gidx_h, gidx_s)]
        )
    ]
    for n in (6, 7, 8, 9, 0, 1, 2, 3, 4, 5):
        loads[n].start()

    bar = pltpu.get_barrier_semaphore()

    def hail_z(i, c):
        pl.semaphore_signal(bar, inc=1, device_id=(s, lax.rem(g + i, NG)), device_id_type=MESH)
        return c

    def hail_p(i, c):
        pl.semaphore_signal(bar, inc=1, device_id=(lax.rem(s + i, NS), g), device_id_type=MESH)
        return c

    lax.fori_loop(1, NG, hail_z, 0)
    lax.fori_loop(1, NS, hail_p, 0)

    def remote(src, dst, ss, rs, dev):
        return pltpu.make_async_remote_copy(
            src_ref=src, dst_ref=dst, send_sem=ss, recv_sem=rs, device_id=dev, device_id_type=MESH
        )

    def z_copy(i, make, ss, rs):
        t = lax.rem(g + i, NG)
        src, dst = make(t)
        return remote(src, dst, ss.at[i], rs.at[i], (s, t))

    def p_copy(i, make, ss, rs):
        t = lax.rem(s + i, NS)
        src, dst = make(t)
        return remote(src, dst, ss.at[i], rs.at[i], (t, g))

    def start_all(copy, n, make, ss, rs):
        def f(i, c):
            copy(i, make, ss, rs).start()
            return c

        lax.fori_loop(1, n, f, 0)

    def recv_all(copy, n, make, ss, rs):
        def f(i, c):
            copy(i, make, ss, rs).wait_recv()
            return c

        lax.fori_loop(1, n, f, 0)

    def sent_all(copy, n, make, ss, rs):
        def f(i, c):
            copy(i, make, ss, rs).wait_send()
            return c

        lax.fori_loop(1, n, f, 0)

    sign = (1, -1)

    def away(n):
        return lax.rem(g + n + NG, NG)

    def kinds(kind, count):
        for p in range(count):
            for way in range(2):
                if kind != 3 or p % 2 == way:
                    yield p, way

    def ag_copy(kind, way, p, slot, ss, rs):
        o = g if kind < 2 else away(-2 * sign[way])
        ref = slot(o, p)
        to = away(sign[way] * (1, 2, 1, 2)[kind])
        return remote(ref, ref, ss.at[kind, way, p], rs.at[kind, way, p], (s, to))

    def gather(count, slot, ss, rs):
        for kind in (1, 0):
            for p, way in kinds(kind, count):
                ag_copy(kind, way, p, slot, ss, rs).start()
        yield
        for p, way in kinds(1, count):
            ag_copy(1, way, p, slot, ss, rs).wait_recv()
            ag_copy(2, way, p, slot, ss, rs).start()
            if p % 2 == way:
                ag_copy(3, way, p, slot, ss, rs).start()
        yield

    def gather_end(count, slot, ss, rs):
        for kind in (0, 2, 3):
            for p, way in kinds(kind, count):
                ag_copy(kind, way, p, slot, ss, rs).wait_recv()

    def gather_sent(count, slot, ss, rs):
        for kind in range(4):
            for p, way in kinds(kind, count):
                ag_copy(kind, way, p, slot, ss, rs).wait_send()

    def rs_copy(kind, way, p, own, stage, recv, ss, rs):
        sg = sign[way]
        src = stage.at[way, p] if kind == 3 else own(away(sg * (3, 4, 1)[kind]), p)
        to = away(sg * (1, 2, 1, 2)[kind])
        return remote(src, recv.at[kind, way, p], ss.at[kind, way, p], rs.at[kind, way, p], (s, to))

    def rs_kinds(kind, count):
        for p in range(count):
            for way in range(2):
                if kind != 1 or p % 2 == way:
                    yield p, way

    def scatter(count, own, stage, recv, ss, rs):
        for kind in (1, 0, 2):
            for p, way in rs_kinds(kind, count):
                rs_copy(kind, way, p, own, stage, recv, ss, rs).start()
        yield
        for p, way in rs_kinds(0, count):
            rs_copy(0, way, p, own, stage, recv, ss, rs).wait_recv()
            v = own(away(2 * sign[way]), p)[...].astype(F32) + recv[0, way, p].astype(F32)
            if p % 2 == way:
                rs_copy(1, way, p, own, stage, recv, ss, rs).wait_recv()
                v = v + recv[1, way, p].astype(F32)
            stage[way, p] = v.astype(BF)
            rs_copy(3, way, p, own, stage, recv, ss, rs).start()
        yield

    def scatter_end(p, own, stage, recv, ss, rs):
        v = own(g, p)[...].astype(F32)
        for kind in (2, 3):
            for way in range(2):
                rs_copy(kind, way, p, own, stage, recv, ss, rs).wait_recv()
                v = v + recv[kind, way, p].astype(F32)
        return v

    def scatter_sent(count, own, stage, recv, ss, rs):
        for kind in range(4):
            for p, way in rs_kinds(kind, count):
                rs_copy(kind, way, p, own, stage, recv, ss, rs).wait_send()

    loads[6].wait()

    def spread(i, c):
        at = pl.ds(pl.multiple_of(i * 128, 128), 128)
        row = jnp.broadcast_to(dsc_v[0:1, at], (128, 128))
        dcol[at, :] = row.T
        return c

    lax.fori_loop(0, NL // 128, spread, 0)
    loads[0].wait()

    def weigh(i, c):
        at = pl.ds(pl.multiple_of(i * 128, 128), 128)
        d = dcol[at, :]
        for n in range(NR // 128):
            cols = slice(n * 128, n * 128 + 128)
            wgt[at, cols] = (res[at, cols] * d).astype(BF)
        return c

    lax.fori_loop(0, NL // 128, weigh, 0)

    for n in (7, 8, 9):
        loads[n].wait()

    def name_blocks(j, x):
        at = jnp.int32(0)
        has = jnp.int32(0)
        for k in range(NCB):
            hit = jnp.where(bidx_s[0, k] == j, jnp.where(cnt_s[0, 0] > k, 1, 0), 0)
            at = jnp.where(hit == 1, k, at)
            has = jnp.where(hit == 1, 1, has)
        ctab[0, j] = at
        ctab[1, j] = has
        return x

    lax.fori_loop(0, NB2, name_blocks, 0)

    loads[1].wait()
    for k in range(NCB):
        v = dot_t(cbas[:, k * CB : (k + 1) * CB], wgt[...])
        crs[2 * k : 2 * k + 2] = v.astype(BF).reshape(2, HB, NR)

    def place(j, x):
        at = ctab[0, j] * 2
        has = ctab[1, j].astype(F32)
        for low in range(2):
            v = (crs[at + low].astype(F32) * has).astype(BF)
            for c in range(NCH):
                own[c, 2 * j + low] = v[:, c * W : (c + 1) * W]
        return x

    lax.fori_loop(0, NB2, place, 0)
    pl.semaphore_wait(bar, NG - 1 + NS - 1)

    def b_all(c):
        return (
            lambda d, p: own.at[c, d * NH + p],
            b_stage.at[c], b_recv.at[c], b_ss.at[c], b_rs.at[c],
        )

    def a_all(c):
        return NH, lambda o, p: rhs2.at[c, o * NH + p], a_ss.at[c], a_rs.at[c]

    def local_tile(i):
        def work():
            if i == 0:
                loads[2].wait()
            local[i * 256 : (i + 1) * 256, :] = dot(linv[i * 256 : (i + 1) * 256, :], wgt[...])

        return work

    def name_slots():
        def f(b, c):
            at = jnp.int32(0)
            has = jnp.int32(0)
            for j in range(MB2):
                hit = gidx_s[0, j] == b
                at = jnp.where(hit, j, at)
                has = jnp.where(hit, 1, has)
            gtab[0, b] = at
            gtab[1, b] = has
            return c

        lax.fori_loop(0, NB3, f, 0)

    def fill_perm(lo, hi):
        def f(b, c):
            k = lax.broadcasted_iota(jnp.int32, (128, 1024), 0)
            n = lax.broadcasted_iota(jnp.int32, (128, 1024), 1)
            want = (k // SL) * 128 + b * SL + k % SL
            at = pl.ds(pl.multiple_of(b * 128, 128), 128)
            perm[at, :] = jnp.where(n == want, 1.0, 0.0).astype(BF)
            return c

        return lambda: lax.fori_loop(lo, hi, f, 0)

    def retile():
        loads[5].wait()
        for q in range(4):
            tstage[q * SL : (q + 1) * SL, :] = l3inv[:, q * 1024 : (q + 1) * 1024]
        moved = dot(tstage[...], perm[...]).astype(BF)
        for m in range(NG):
            for q in range(4):
                v = moved[q * SL : (q + 1) * SL, m * 128 : (m + 1) * 128]
                tsend[m, :, q * 128 : (q + 1) * 128] = v
        tile[g] = tsend[g]

    def t_make(t):
        return tsend.at[t], tile.at[g]

    work = iter([local_tile(i) for i in range(4)] + [
        name_slots, fill_perm(0, 4), fill_perm(4, 8), retile
    ])

    def phase_w(c):
        next(work)()

    b_steps = [scatter(NH, *b_all(c)) for c in range(NCH)]
    a_steps = [gather(*a_all(c)) for c in range(NCH)]

    def phase_b(c):
        next(b_steps[c])

    def phase_a(c):
        next(a_steps[c])

    def d_all(c):
        return (
            lambda d, p: part.at[c, pl.ds(p * PJ, PJ), d],
            d_stage.at[c], d_recv.at[c], d_ss.at[c], d_rs.at[c],
        )

    d_steps = [scatter(MB2 // PJ, *d_all(c)) for c in range(NCH)]

    def phase_d(c):
        for q in range(NH):
            rhs2[c, g * NH + q] = scatter_end(q, *b_all(c)).astype(BF)
        if c == 0:
            loads[3].wait()
            loads[4].wait()
        mine = rhs2[c, pl.ds(g * NH, NH)].reshape(OWN2, W)
        for n in range(MB2 // 2):
            v = dot_t(l2bas[:, n * 256 : (n + 1) * 256], mine).astype(BF)
            part[c, 2 * n : 2 * n + 2] = v.reshape(2, NG, SL, W)
        next(d_steps[c])

    def phase_q(c):
        next(d_steps[c])

    def phase_s(c):
        gather_end(*a_all(c))
        l2loc[:, c * W : (c + 1) * W] = dot(l2inv[...], rhs2[c].reshape(NB2 * CB, W))

    def phase_t(c):
        start_all(z_copy, NG, t_make, t_ss, t_rs)

    def e_make(c):
        return lambda t: (dense.at[c, t], e_recv.at[c, s])

    def f_make(c):
        return lambda t: (xall.at[c, s], xall.at[c, s])

    def h_make(c):
        return lambda t: (hsend.at[c, t], h_recv.at[c, g])

    def i_make(c):
        return lambda t: (yall.at[c, s], yall.at[c, s])

    def j_all(c):
        return (
            MB2 // PJ, lambda o, p: lifted.at[c, pl.ds(p * PJ, PJ), o], j_ss.at[c], j_rs.at[c]
        )

    def l_all(c):
        return NH, lambda o, p: sol2.at[c, o * NH + p], l_ss.at[c], l_rs.at[c]

    j_steps = [gather(*j_all(c)) for c in range(NCH)]
    l_steps = [gather(*l_all(c)) for c in range(NCH)]

    def phase_t(c):
        start_all(z_copy, NG, t_make, t_ss, t_rs)

    def e_make(c):
        return lambda t: (dense.at[c, t], e_recv.at[c, s])

    def f_make(c):
        return lambda t: (xall.at[c, s], xall.at[c, s])

    def h_make(c):
        return lambda t: (hsend.at[c, t], h_recv.at[c, g])

    def i_make(c):
        return lambda t: (yall.at[c, s], yall.at[c, s])

    def j_make(c):
        return lambda t: (picked.at[c], lifted.at[c, :, g])

    def l_slot(c):
        return lambda o, q: sol2.at[c, o * NH + q]

    def phase_e(c):
        for p in range(MB2 // PJ):
            ssum[c, p * PJ : (p + 1) * PJ] = scatter_end(p, *d_all(c))

        def f(b, x):
            dense[c, b] = (ssum[c, gtab[0, b]] * gtab[1, b].astype(F32)).astype(BF)
            return x

        lax.fori_loop(0, NB3, f, 0)
        start_all(p_copy, NS, e_make(c), e_ss.at[c], e_rs.at[c])
        e_recv[c, s] = dense[c, s]

    def phase_f(c):
        recv_all(p_copy, NS, e_make(c), e_ss.at[c], e_rs.at[c])

        def f(b, v):
            return v + e_recv[c, b].astype(F32)

        xall[c, s] = lax.fori_loop(0, NS, f, jnp.zeros((SL, W), F32)).astype(BF)
        start_all(p_copy, NS, f_make(c), f_ss.at[c], f_rs.at[c])

    def phase_h(c):
        if c == 0:
            recv_all(z_copy, NG, t_make, t_ss, t_rs)
        recv_all(p_copy, NS, f_make(c), f_ss.at[c], f_rs.at[c])
        v = dot(tile[...].reshape(CB, NB3 * SL), xall[c].reshape(NB3 * SL, W))
        hsend[c] = v.astype(BF).reshape(NG, SL, W)
        start_all(z_copy, NG, h_make(c), h_ss.at[c], h_rs.at[c])
        h_recv[c, g] = hsend[c, g]

    def phase_i(c):
        recv_all(z_copy, NG, h_make(c), h_ss.at[c], h_rs.at[c])
        v = h_recv[c, 0].astype(F32)
        for m in range(1, NG):
            v = v + h_recv[c, m].astype(F32)
        yall[c, s] = v.astype(BF)
        start_all(p_copy, NS, i_make(c), i_ss.at[c], i_rs.at[c])

    def phase_j(c):
        recv_all(p_copy, NS, i_make(c), i_ss.at[c], i_rs.at[c])
        for j in range(MB2):
            lifted[c, j, g] = yall[c, gidx_s[0, j]]
        next(j_steps[c])

    def phase_g(c):
        next(j_steps[c])

    def phase_k(c):
        gather_end(*j_all(c))
        cols = slice(c * W, (c + 1) * W)
        v = l2loc[:, cols] + dot(l2bas[...], lifted[c].reshape(MB2 * CB, W))
        sol2[c, pl.ds(g * NH, NH)] = v.astype(BF).reshape(NH, HB, W)

    def phase_l(c):
        next(l_steps[c])

    def n_copy(c, f):
        dev = (
            (s, lax.rem(g + NG - 1, NG)),
            (s, lax.rem(g + 1, NG)),
            (lax.rem(s + NS - 1, NS), g),
            (lax.rem(s + 1, NS), g),
        )[f]
        return remote(fsend.at[c, f], f_recv.at[c, f ^ 1], n_ss.at[c, f], n_rs.at[c, f ^ 1], dev)

    def total_rows(c, lo, n):
        v = dot(cbas[lo : lo + n, :], chosen[c])
        cols = slice(c * W, (c + 1) * W)
        v = v + local[lo : lo + n, cols]
        d = dcol[lo : lo + n, :]
        if W > 128:
            d = jnp.concatenate([d] * (W // 128), axis=1)
        return v * d

    def phase_n(c):
        gather_end(*l_all(c))
        for k in range(NCB):
            for low in range(2):
                v = sol2[c, bidx_s[0, k] * 2 + low].astype(F32) * (cnt_s[0, 0] > k).astype(F32)
                at = k * CB + low * HB
                chosen[c, at : at + HB, :] = v.astype(BF)
        cols = slice(c * W, (c + 1) * W)
        for f in range(4):
            v = total_rows(c, f * CB, CB)
            out_ref[f * CB : (f + 1) * CB, cols] = v
            fsend[c, f] = v.astype(BF)
            n_copy(c, f).start()

    def phase_r(c):
        cols = slice(c * W, (c + 1) * W)
        for f in range(2, 4):
            out_ref[f * 256 : (f + 1) * 256, cols] = total_rows(c, f * 256, 256)

    def phase_o(c):
        cols = slice(c * W, (c + 1) * W)
        inside = (g > 0, g < NG - 1, s > 0, s < NS - 1)
        for f in range(4):
            n_copy(c, f ^ 1).wait_recv()
            at = slice(f * CB, (f + 1) * CB)
            v = f_recv[c, f].astype(F32) * inside[f].astype(F32)
            out_ref[at, cols] = out_ref[at, cols] + v

    phases = dict(
        a=phase_a, b=phase_b, w=phase_w, d=phase_d, s=phase_s, e=phase_e, f=phase_f, h=phase_h, i=phase_i,
        j=phase_j, g=phase_g, q=phase_q, t=phase_t, k=phase_k, l=phase_l, n=phase_n, r=phase_r, o=phase_o,
    )
    for name in ORDER:
        phases[name[0]](int(name[1]))

    sent_all(z_copy, NG, t_make, t_ss, t_rs)
    for c in range(NCH):
        scatter_sent(NH, *b_all(c))
        gather_sent(*a_all(c))
        scatter_sent(MB2 // PJ, *d_all(c))
        sent_all(p_copy, NS, e_make(c), e_ss.at[c], e_rs.at[c])
        sent_all(p_copy, NS, f_make(c), f_ss.at[c], f_rs.at[c])
        sent_all(z_copy, NG, h_make(c), h_ss.at[c], h_rs.at[c])
        sent_all(p_copy, NS, i_make(c), i_ss.at[c], i_rs.at[c])
        gather_sent(*j_all(c))
        gather_sent(*l_all(c))
        for f in range(4):
            n_copy(c, f).wait_send()


def local(
    residual,
    dscale,
    local_inverse,
    coarse_basis,
    block_counts,
    block_index,
    level2_inverse,
    level2_basis,
    group_index,
    level3_inverse,
):
    vm = pltpu.VMEM
    dma = pltpu.SemaphoreType.DMA
    vmem = pl.BlockSpec(memory_space=pltpu.VMEM)
    hbm = pl.BlockSpec(memory_space=pltpu.HBM)
    ring_sem = dma((NCH, 4, 2, NH))
    piece_sem = dma((NCH, 4, 2, MB2 // PJ))
    z_sem = dma((NCH, NG))
    p_sem = dma((NCH, NS))
    scratch = [
        pltpu.SMEM((1, 1), jnp.int32), pltpu.SMEM((1, NCB), jnp.int32), pltpu.SMEM((1, MB2), jnp.int32),
        vm((1, NL), F32), vm((NL, NR), F32), vm((NL, NL), BF), vm((NL, NCB * CB), BF), vm((OWN2, NB2 * CB), BF),
        vm((OWN2, MB2 * CB), BF), vm((SL, NB3 * CB), BF), dma((10,)),
        vm((NL, 128), F32), vm((NL, NR), BF), vm((NL, NR), F32), vm((1024, 1024), BF),
        vm((4 * SL, 1024), BF), vm((NG, SL, NB3 * SL), BF), vm((NG, SL, NB3 * SL), BF),
        dma((NG,)), dma((NG,)),
        pltpu.SMEM((2, NB2), jnp.int32), pltpu.SMEM((2, NB3), jnp.int32),
        vm((2 * NCB, HB, NR), BF), vm((NCH, NG * NH, HB, W), BF), vm((NCH, 2, NH, HB, W), BF),
        vm((NCH, 4, 2, NH, HB, W), BF), ring_sem, ring_sem,
        vm((NCH, NG * NH, HB, W), BF), ring_sem, ring_sem, vm((OWN2, NR), F32), vm((NCH, MB2, NG, SL, W), BF),
        vm((NCH, 2, MB2 // PJ, PJ, SL, W), BF), vm((NCH, 4, 2, MB2 // PJ, PJ, SL, W), BF), piece_sem, piece_sem,
        vm((NCH, MB2, SL, W), F32), vm((NCH, NB3, SL, W), BF), vm((NCH, NS, SL, W), BF), p_sem, p_sem,
        vm((NCH, NB3, SL, W), BF), p_sem, p_sem,
        vm((NCH, NG, SL, W), BF), vm((NCH, NG, SL, W), BF), z_sem, z_sem,
        vm((NCH, NB3, SL, W), BF), p_sem, p_sem,
        vm((NCH, MB2, NG, SL, W), BF), piece_sem, piece_sem,
        vm((NCH, NG * NH, HB, W), BF), ring_sem, ring_sem,
        vm((NCH, NCB * CB, W), BF), vm((NCH, 4, CB, W), BF), vm((NCH, 4, CB, W), BF),
        dma((NCH, 4)), dma((NCH, 4)),
    ]
    out = pl.pallas_call(
        kernel,
        out_shape=jax.ShapeDtypeStruct((NL, NR), F32),
        in_specs=[hbm] * 10,
        out_specs=vmem,
        scratch_shapes=scratch,
        name="bddc",
        compiler_params=pltpu.CompilerParams(
            collective_id=0, has_side_effects=True, vmem_limit_bytes=60 << 20
        ),
    )(
        block_counts.reshape(1, 1), block_index, group_index, dscale, residual[0], local_inverse[0],
        coarse_basis[0], level2_inverse[0], level2_basis[0], level3_inverse,
    )
    return out[None]


def solution(mesh):
    return jax.shard_map(
        local,
        mesh=mesh,
        in_specs=(
            P(("sub", "grp"), None, None),
            P(("sub", "grp"), None),
            P(("sub", "grp"), None, None),
            P(("sub", "grp"), None, None),
            P(("sub", "grp")),
            P(("sub", "grp"), None),
            P("sub", "grp", None),
            P("sub", "grp", None),
            P("sub", None),
            P(("sub", "grp"), None),
        ),
        out_specs=P(("sub", "grp"), None, None),
        check_vma=False,
    )
```

time: 120 us -> 95.8 us (0.80)
  Pallas kernels: 109 us -> 92.7 us
  local copies, waits for them, and re-layouts: 9.87 us -> 2.26 us
    pallas_call x1, Pallas kernels: 109 us -> 92.7 us  [local(): pl.pallas_call(kernel, out_shape=jax.ShapeDtypeStruct((NL, NR), F32), in_...]
    unnamed x19 -> x1, local copies, waits for them, and re-layouts: 9.87 us -> 2.26 us
where the time goes in v2:
time: 95.8 us; the launch traced here: 95.7 us
  Pallas kernels  92.7 us (97%)
  local copies, waits for them, and re-layouts  2.26 us (2%)
    pallas_call x1, Pallas kernels, local(): pl.pallas_call(kernel, out_shape=jax.ShapeDtypeStruct((NL, NR), F32), in_...  92.7 us
    unnamed x1, local copies, waits for them, and re-layouts  2.26 us

profile of v2, /device:TPU:1, one launch (start us, length us, event | category | flops | bytes accessed | tf_op | source)
XLA Modules:
  0.0 95.7 jit_solution(3911812432134547610)
XLA Ops:
  0.7 92.7 %bddc.1 = f32[1024,256]{1,0:T(8,128)} custom-call(s32[1,1]{1,0:T(1,128)} %bitcast.7.cnt_h, s32[1,3]{1,0:T(1,128)} %bidx_h.1, s32[1,8]{1,0:T(1,128)} %gidx_h.1, f32[1,1024]{1,0:T(1,128)} %dsc_h.1, f32[1024,256]{1,0:T(8,128)} %bitcast.10, bf16[1024,1024]{1,0:T(8,128)(2,1)} %bitcast.9, bf16[1024,384]{1,0:T(8,128)(2,1)} %bitcast.11, bf16[192,1536]{1,0:T(8,128)(2,1)} %bitcast.12, ...), custom_call_target="tpu_custom_call" | custom-call | tf_op jit(solution)/shard_map/bddc/pallas_call | solution.py:566
  93.4 2.3 %copy.13 = f32[1,1024,256]{2,1,0:T(8,128)} copy(f32[1,1024,256]{2,1,0:T(8,128)} %bitcast.8) | data formatting | bytes 2097152

commit v3 on v2

--- a/solution.py
+++ b/solution.py
@@ -18,15 +18,16 @@
 NB3 = 32
 SL = CB // NG
 OWN2 = NB2 * CB // NG
-HB = CB // 2
+QB = 2
+HB = CB // QB
 NH = OWN2 // HB
 NCH = 1
 W = NR // NCH
 PJ = 2
 
 ORDER = (
-    "b0", "w0", "w0", "w0", "w0", "w0", "b0", "w0", "w0", "w0", "d0", "q0", "e0", "t0", "f0", "a0",
-    "h0", "a0", "i0", "j0", "g0", "s0", "k0", "l0", "l0", "n0", "r0", "o0",
+    "b0", "w0", "w0", "w0", "w0", "w0", "b0", "w0", "w0", "w0", "d0", "q0", "e0", "t0", "a0", "f0", "a0",
+    "h0", "i0", "j0", "s0", "g0", "x0", "k0", "l0", "y0", "l0", "n0", "r0", "o0",
 )
 
 MESH = pl.DeviceIdType.MESH
@@ -67,7 +68,7 @@
              (l3inv_h, l3inv), (dsc_h, dsc_v), (cnt_h, cnt_s), (bidx_h, bidx_s), (gidx_h, gidx_s)]
         )
     ]
-    for n in (6, 7, 8, 9, 0, 1, 2, 3, 4, 5):
+    for n in (6, 0, 1, 7, 8, 9):
         loads[n].start()
 
     bar = pltpu.get_barrier_semaphore()
@@ -88,36 +89,26 @@
             src_ref=src, dst_ref=dst, send_sem=ss, recv_sem=rs, device_id=dev, device_id_type=MESH
         )
 
-    def z_copy(i, make, ss, rs):
-        t = lax.rem(g + i, NG)
-        src, dst = make(t)
-        return remote(src, dst, ss.at[i], rs.at[i], (s, t))
-
-    def p_copy(i, make, ss, rs):
-        t = lax.rem(s + i, NS)
-        src, dst = make(t)
-        return remote(src, dst, ss.at[i], rs.at[i], (t, g))
-
-    def start_all(copy, n, make, ss, rs):
+    def z_start(make, ss, rs):
         def f(i, c):
-            copy(i, make, ss, rs).start()
+            t = lax.rem(g + i, NG)
+            src, dst = make(t)
+            remote(src, dst, ss, rs, (s, t)).start()
             return c
 
-        lax.fori_loop(1, n, f, 0)
-
-    def recv_all(copy, n, make, ss, rs):
+        lax.fori_loop(1, NG, f, 0)
+
+    def p_start(make, ss, rs):
         def f(i, c):
-            copy(i, make, ss, rs).wait_recv()
+            t = lax.rem(s + i, NS)
+            src, dst = make(t)
+            remote(src, dst, ss, rs, (t, g)).start()
             return c
 
-        lax.fori_loop(1, n, f, 0)
-
-    def sent_all(copy, n, make, ss, rs):
-        def f(i, c):
-            copy(i, make, ss, rs).wait_send()
-            return c
-
-        lax.fori_loop(1, n, f, 0)
+        lax.fori_loop(1, NS, f, 0)
+
+    def all_of(some, ss, rs):
+        return remote(some, some, ss, rs, (s, lax.rem(g + 1, NG)))
 
     sign = (1, -1)
 
@@ -219,6 +210,9 @@
 
     lax.fori_loop(0, NL // 128, weigh, 0)
 
+    for n in (2, 3, 4, 5):
+        loads[n].start()
+
     for n in (7, 8, 9):
         loads[n].wait()
 
@@ -238,15 +232,15 @@
     loads[1].wait()
     for k in range(NCB):
         v = dot_t(cbas[:, k * CB : (k + 1) * CB], wgt[...])
-        crs[2 * k : 2 * k + 2] = v.astype(BF).reshape(2, HB, NR)
+        crs[QB * k : QB * k + QB] = v.astype(BF).reshape(QB, HB, NR)
 
     def place(j, x):
-        at = ctab[0, j] * 2
+        at = ctab[0, j] * QB
         has = ctab[1, j].astype(F32)
-        for low in range(2):
+        for low in range(QB):
             v = (crs[at + low].astype(F32) * has).astype(BF)
             for c in range(NCH):
-                own[c, 2 * j + low] = v[:, c * W : (c + 1) * W]
+                own[c, QB * j + low] = v[:, c * W : (c + 1) * W]
         return x
 
     lax.fori_loop(0, NB2, place, 0)
@@ -351,9 +345,6 @@
         gather_end(*a_all(c))
         l2loc[:, c * W : (c + 1) * W] = dot(l2inv[...], rhs2[c].reshape(NB2 * CB, W))
 
-    def phase_t(c):
-        start_all(z_copy, NG, t_make, t_ss, t_rs)
-
     def e_make(c):
         return lambda t: (dense.at[c, t], e_recv.at[c, s])
 
@@ -365,6 +356,21 @@
 
     def i_make(c):
         return lambda t: (yall.at[c, s], yall.at[c, s])
+
+    def e_all(c):
+        return all_of(e_recv.at[c, pl.ds(1, NS - 1)], e_ss.at[c], e_rs.at[c])
+
+    def f_all(c):
+        return all_of(xall.at[c, pl.ds(1, NS - 1)], f_ss.at[c], f_rs.at[c])
+
+    def i_all(c):
+        return all_of(yall.at[c, pl.ds(1, NS - 1)], i_ss.at[c], i_rs.at[c])
+
+    def h_all(c):
+        return all_of(h_recv.at[c, pl.ds(1, NG - 1)], h_ss.at[c], h_rs.at[c])
+
+    def t_all():
+        return all_of(tile.at[pl.ds(1, NG - 1)], t_ss, t_rs)
 
     def j_all(c):
         return (
@@ -378,7 +384,7 @@
     l_steps = [gather(*l_all(c)) for c in range(NCH)]
 
     def phase_t(c):
-        start_all(z_copy, NG, t_make, t_ss, t_rs)
+        z_start(t_make, t_ss, t_rs)
 
     def e_make(c):
         return lambda t: (dense.at[c, t], e_recv.at[c, s])
@@ -407,37 +413,37 @@
             return x
 
         lax.fori_loop(0, NB3, f, 0)
-        start_all(p_copy, NS, e_make(c), e_ss.at[c], e_rs.at[c])
+        p_start(e_make(c), e_ss.at[c], e_rs.at[c])
         e_recv[c, s] = dense[c, s]
 
     def phase_f(c):
-        recv_all(p_copy, NS, e_make(c), e_ss.at[c], e_rs.at[c])
+        e_all(c).wait_recv()
 
         def f(b, v):
             return v + e_recv[c, b].astype(F32)
 
         xall[c, s] = lax.fori_loop(0, NS, f, jnp.zeros((SL, W), F32)).astype(BF)
-        start_all(p_copy, NS, f_make(c), f_ss.at[c], f_rs.at[c])
+        p_start(f_make(c), f_ss.at[c], f_rs.at[c])
 
     def phase_h(c):
         if c == 0:
-            recv_all(z_copy, NG, t_make, t_ss, t_rs)
-        recv_all(p_copy, NS, f_make(c), f_ss.at[c], f_rs.at[c])
+            t_all().wait_recv()
+        f_all(c).wait_recv()
         v = dot(tile[...].reshape(CB, NB3 * SL), xall[c].reshape(NB3 * SL, W))
         hsend[c] = v.astype(BF).reshape(NG, SL, W)
-        start_all(z_copy, NG, h_make(c), h_ss.at[c], h_rs.at[c])
+        z_start(h_make(c), h_ss.at[c], h_rs.at[c])
         h_recv[c, g] = hsend[c, g]
 
     def phase_i(c):
-        recv_all(z_copy, NG, h_make(c), h_ss.at[c], h_rs.at[c])
+        h_all(c).wait_recv()
         v = h_recv[c, 0].astype(F32)
         for m in range(1, NG):
             v = v + h_recv[c, m].astype(F32)
         yall[c, s] = v.astype(BF)
-        start_all(p_copy, NS, i_make(c), i_ss.at[c], i_rs.at[c])
+        p_start(i_make(c), i_ss.at[c], i_rs.at[c])
 
     def phase_j(c):
-        recv_all(p_copy, NS, i_make(c), i_ss.at[c], i_rs.at[c])
+        i_all(c).wait_recv()
         for j in range(MB2):
             lifted[c, j, g] = yall[c, gidx_s[0, j]]
         next(j_steps[c])
@@ -453,6 +459,18 @@
 
     def phase_l(c):
         next(l_steps[c])
+
+    def phase_x(c):
+        scatter_sent(NH, *b_all(c))
+        scatter_sent(MB2 // PJ, *d_all(c))
+        if c == 0:
+            t_all().wait_send()
+        for each in (e_all, f_all, h_all, i_all):
+            each(c).wait_send()
+        gather_sent(*a_all(c))
+
+    def phase_y(c):
+        gather_sent(*j_all(c))
 
     def n_copy(c, f):
         dev = (
@@ -475,8 +493,8 @@
     def phase_n(c):
         gather_end(*l_all(c))
         for k in range(NCB):
-            for low in range(2):
-                v = sol2[c, bidx_s[0, k] * 2 + low].astype(F32) * (cnt_s[0, 0] > k).astype(F32)
+            for low in range(QB):
+                v = sol2[c, bidx_s[0, k] * QB + low].astype(F32) * (cnt_s[0, 0] > k).astype(F32)
                 at = k * CB + low * HB
                 chosen[c, at : at + HB, :] = v.astype(BF)
         cols = slice(c * W, (c + 1) * W)
@@ -502,21 +520,12 @@
 
     phases = dict(
         a=phase_a, b=phase_b, w=phase_w, d=phase_d, s=phase_s, e=phase_e, f=phase_f, h=phase_h, i=phase_i,
-        j=phase_j, g=phase_g, q=phase_q, t=phase_t, k=phase_k, l=phase_l, n=phase_n, r=phase_r, o=phase_o,
+        j=phase_j, g=phase_g, q=phase_q, t=phase_t, x=phase_x, y=phase_y, k=phase_k, l=phase_l, n=phase_n, r=phase_r, o=phase_o,
     )
     for name in ORDER:
         phases[name[0]](int(name[1]))
 
-    sent_all(z_copy, NG, t_make, t_ss, t_rs)
     for c in range(NCH):
-        scatter_sent(NH, *b_all(c))
-        gather_sent(*a_all(c))
-        scatter_sent(MB2 // PJ, *d_all(c))
-        sent_all(p_copy, NS, e_make(c), e_ss.at[c], e_rs.at[c])
-        sent_all(p_copy, NS, f_make(c), f_ss.at[c], f_rs.at[c])
-        sent_all(z_copy, NG, h_make(c), h_ss.at[c], h_rs.at[c])
-        sent_all(p_copy, NS, i_make(c), i_ss.at[c], i_rs.at[c])
-        gather_sent(*j_all(c))
         gather_sent(*l_all(c))
         for f in range(4):
             n_copy(c, f).wait_send()
@@ -540,24 +549,23 @@
     hbm = pl.BlockSpec(memory_space=pltpu.HBM)
     ring_sem = dma((NCH, 4, 2, NH))
     piece_sem = dma((NCH, 4, 2, MB2 // PJ))
-    z_sem = dma((NCH, NG))
-    p_sem = dma((NCH, NS))
+    one_sem = dma((NCH,))
     scratch = [
         pltpu.SMEM((1, 1), jnp.int32), pltpu.SMEM((1, NCB), jnp.int32), pltpu.SMEM((1, MB2), jnp.int32),
         vm((1, NL), F32), vm((NL, NR), F32), vm((NL, NL), BF), vm((NL, NCB * CB), BF), vm((OWN2, NB2 * CB), BF),
         vm((OWN2, MB2 * CB), BF), vm((SL, NB3 * CB), BF), dma((10,)),
         vm((NL, 128), F32), vm((NL, NR), BF), vm((NL, NR), F32), vm((1024, 1024), BF),
         vm((4 * SL, 1024), BF), vm((NG, SL, NB3 * SL), BF), vm((NG, SL, NB3 * SL), BF),
-        dma((NG,)), dma((NG,)),
+        dma(()), dma(()),
         pltpu.SMEM((2, NB2), jnp.int32), pltpu.SMEM((2, NB3), jnp.int32),
-        vm((2 * NCB, HB, NR), BF), vm((NCH, NG * NH, HB, W), BF), vm((NCH, 2, NH, HB, W), BF),
+        vm((QB * NCB, HB, NR), BF), vm((NCH, NG * NH, HB, W), BF), vm((NCH, 2, NH, HB, W), BF),
         vm((NCH, 4, 2, NH, HB, W), BF), ring_sem, ring_sem,
         vm((NCH, NG * NH, HB, W), BF), ring_sem, ring_sem, vm((OWN2, NR), F32), vm((NCH, MB2, NG, SL, W), BF),
         vm((NCH, 2, MB2 // PJ, PJ, SL, W), BF), vm((NCH, 4, 2, MB2 // PJ, PJ, SL, W), BF), piece_sem, piece_sem,
-        vm((NCH, MB2, SL, W), F32), vm((NCH, NB3, SL, W), BF), vm((NCH, NS, SL, W), BF), p_sem, p_sem,
-        vm((NCH, NB3, SL, W), BF), p_sem, p_sem,
-        vm((NCH, NG, SL, W), BF), vm((NCH, NG, SL, W), BF), z_sem, z_sem,
-        vm((NCH, NB3, SL, W), BF), p_sem, p_sem,
+        vm((NCH, MB2, SL, W), F32), vm((NCH, NB3, SL, W), BF), vm((NCH, NS, SL, W), BF), one_sem, one_sem,
+        vm((NCH, NB3, SL, W), BF), one_sem, one_sem,
+        vm((NCH, NG, SL, W), BF), vm((NCH, NG, SL, W), BF), one_sem, one_sem,
+        vm((NCH, NB3, SL, W), BF), one_sem, one_sem,
         vm((NCH, MB2, NG, SL, W), BF), piece_sem, piece_sem,
         vm((NCH, NG * NH, HB, W), BF), ring_sem, ring_sem,
         vm((NCH, NCB * CB, W), BF), vm((NCH, 4, CB, W), BF), vm((NCH, 4, CB, W), BF),

time: 95.8 us -> 92.2 us (0.962)
  Pallas kernels: 92.7 us -> 89.2 us
    pallas_call x1, Pallas kernels: 92.7 us -> 89.2 us  [local(): pl.pallas_call(kernel, out_shape=jax.ShapeDtypeStruct((NL, NR), F32), in_...]
where the time goes in v3:
time: 92.2 us; the launch traced here: 92.1 us
  Pallas kernels  89.2 us (97%)
  local copies, waits for them, and re-layouts  2.26 us (2%)
    pallas_call x1, Pallas kernels, local(): pl.pallas_call(kernel, out_shape=jax.ShapeDtypeStruct((NL, NR), F32), in_...  89.2 us
    unnamed x1, local copies, waits for them, and re-layouts  2.26 us

profile of v3, /device:TPU:1, one launch (start us, length us, event | category | flops | bytes accessed | tf_op | source)
XLA Modules:
  0.0 92.1 jit_solution(5269976684959237594)
XLA Ops:
  0.7 89.2 %bddc.1 = f32[1024,256]{1,0:T(8,128)} custom-call(s32[1,1]{1,0:T(1,128)} %bitcast.7.cnt_h, s32[1,3]{1,0:T(1,128)} %bidx_h.1, s32[1,8]{1,0:T(1,128)} %gidx_h.1, f32[1,1024]{1,0:T(1,128)} %dsc_h.1, f32[1024,256]{1,0:T(8,128)} %bitcast.10, bf16[1024,1024]{1,0:T(8,128)(2,1)} %bitcast.9, bf16[1024,384]{1,0:T(8,128)(2,1)} %bitcast.11, bf16[192,1536]{1,0:T(8,128)(2,1)} %bitcast.12, ...), custom_call_target="tpu_custom_call" | custom-call | tf_op jit(solution)/shard_map/bddc/pallas_call | solution.py:574
  89.8 2.3 %copy.13 = f32[1,1024,256]{2,1,0:T(8,128)} copy(f32[1,1024,256]{2,1,0:T(8,128)} %bitcast.8) | data formatting | bytes 2097152

commit v4 on v3

--- a/solution.py
+++ b/solution.py
@@ -18,7 +18,7 @@
 NB3 = 32
 SL = CB // NG
 OWN2 = NB2 * CB // NG
-QB = 2
+QB = 4
 HB = CB // QB
 NH = OWN2 // HB
 NCH = 1

time: 92.2 us -> 92 us (level)
  no operation moved by 1% of the time
where the time goes in v4:
time: 92 us; the launch traced here: 91.8 us
  Pallas kernels  88.9 us (97%)
  local copies, waits for them, and re-layouts  2.26 us (2%)
    pallas_call x1, Pallas kernels, local(): pl.pallas_call(kernel, out_shape=jax.ShapeDtypeStruct((NL, NR), F32), in_...  88.9 us
    unnamed x1, local copies, waits for them, and re-layouts  2.26 us

profile of v4, /device:TPU:1, one launch (start us, length us, event | category | flops | bytes accessed | tf_op | source)
XLA Modules:
  0.0 91.8 jit_solution(15169640933108684631)
XLA Ops:
  0.7 88.9 %bddc.1 = f32[1024,256]{1,0:T(8,128)} custom-call(s32[1,1]{1,0:T(1,128)} %bitcast.7.cnt_h, s32[1,3]{1,0:T(1,128)} %bidx_h.1, s32[1,8]{1,0:T(1,128)} %gidx_h.1, f32[1,1024]{1,0:T(1,128)} %dsc_h.1, f32[1024,256]{1,0:T(8,128)} %bitcast.10, bf16[1024,1024]{1,0:T(8,128)(2,1)} %bitcast.9, bf16[1024,384]{1,0:T(8,128)(2,1)} %bitcast.11, bf16[192,1536]{1,0:T(8,128)(2,1)} %bitcast.12, ...), custom_call_target="tpu_custom_call" | custom-call | tf_op jit(solution)/shard_map/bddc/pallas_call | solution.py:574
  89.6 2.3 %copy.13 = f32[1,1024,256]{2,1,0:T(8,128)} copy(f32[1,1024,256]{2,1,0:T(8,128)} %bitcast.8) | data formatting | bytes 2097152
